TPU v7x, 256 devices: a whole 4x4x8 slice. The times are simulated.
256 devices in a mesh: grp: 8 (over x, y_hi), ing: 32 (over y_lo, z, core).
Axes of the slice: x: 4, y: 4 (y_hi: 2, y_lo: 2; y = y_hi * 2 + y_lo), z: 8, core: 2. Of those that a mesh axis runs over, the one named last changes fastest.
Arguments:
- image_emb: float32 [32768, 1152], P(('grp', 'ing')), may hold values from -22 to 22
- text_emb: float32 [32768, 1152], P(('grp', 'ing')), may hold values from -22 to 22
- logit_scale: float32 [1], replicated, may hold values from 5 to 15
- logit_bias: float32 [1], replicated, may hold values from -3 to -1
Outputs:
- row_loss: float32 [32768], P(('grp', 'ing'))
- image_grad: float32 [32768, 1152], P(('grp', 'ing'))
- text_grad: float32 [32768, 1152], P(('grp', 'ing'))
All inputs are finite; a program needn't handle non-finite values.
Results may differ from a plain program's by a relative error of at most 0.005.
Values may be sent and summed in bfloat16 or wider, within the bound.
A program may use at most 128 MiB of HBM per device.

v0:
```python
import jax
import jax.numpy as jnp
from jax import lax
from jax.sharding import PartitionSpec as P

STEPS = 2


EPSILON = 1e-06


def from_behind(value, axis, steps):
    count = lax.axis_size(axis)
    pairs = [(source, (source + steps) % count) for source in range(count)]
    return lax.ppermute(value, axis, pairs)


def normalize(raw_rows):
    norms = jnp.sqrt(jnp.sum(raw_rows * raw_rows, axis=1, keepdims=True) + EPSILON)
    return (raw_rows / norms, norms)


def restore(unit_grad, unit_rows, norms):
    return (unit_grad - unit_rows * jnp.sum(unit_rows * unit_grad, axis=1, keepdims=True)) / norms


def first_contract(left_side, right_side):
    return lax.dot_general(
        left_side, right_side, (((0,), (0,)), ((), ())), preferred_element_type=jnp.float32
    )


def on_device(image_emb, text_emb, logit_scale, logit_bias):
    unit_img, norm_img = normalize(image_emb)
    unit_txt, norm_txt = normalize(text_emb)
    image_low = unit_img.astype(jnp.bfloat16)
    text_low = unit_txt.astype(jnp.bfloat16)
    local_rows = image_emb.shape[0]
    group_rows = local_rows * lax.axis_size("ing")
    position = lax.axis_index("ing")
    scale_value = logit_scale[0]
    bias_value = logit_bias[0]
    columns = jnp.arange(group_rows, dtype=jnp.int32)
    row_ids = position * local_rows + jnp.arange(local_rows, dtype=jnp.int32)
    labels_own = jnp.where(row_ids[:, None] == columns[None, :], 1.0, -1.0).astype(jnp.float32)
    losses = jnp.zeros((local_rows,), jnp.float32)
    image_acc = jnp.zeros(image_emb.shape, jnp.float32)
    running = jnp.zeros(text_emb.shape, jnp.float32)
    text_block = lax.all_gather(text_low, "ing", axis=0, tiled=True)
    for cycle_step in range(STEPS):
        if cycle_step > 0:
            text_block = from_behind(text_block, "grp", 1)
        logits = (
            scale_value * jnp.dot(image_low, text_block.T, preferred_element_type=jnp.float32)
            + bias_value
        )
        labels = labels_own if cycle_step == 0 else -1.0
        losses = losses + jnp.sum(jax.nn.softplus(-labels * logits), axis=1)
        coefficient = (-labels * jax.nn.sigmoid(-labels * logits)).astype(jnp.bfloat16)
        image_acc = image_acc + jnp.dot(coefficient, text_block, preferred_element_type=jnp.float32)
        partial_sum = first_contract(coefficient, image_low)
        own_grads = lax.psum_scatter(partial_sum, "ing", scatter_dimension=0, tiled=True)
        if cycle_step > 0:
            running = from_behind(running, "grp", 1)
        running = running + own_grads
    text_acc = from_behind(running, "grp", 1 - STEPS)
    row_loss = losses / (STEPS * group_rows)
    image_grad = restore(scale_value * image_acc, unit_img, norm_img)
    text_grad = restore(scale_value * text_acc, unit_txt, norm_txt)
    return (row_loss, image_grad, text_grad)


def solution(mesh):
    placed = (P(("grp", "ing"), None), P(("grp", "ing"), None), P(), P())
    return jax.shard_map(
        on_device,
        mesh=mesh,
        in_specs=placed,
        out_specs=(P(("grp", "ing")), P(("grp", "ing"), None), P(("grp", "ing"), None)),
        check_vma=False,
    )
```

profile of v0, /device:TPU:1, one launch (start us, length us, event | category | flops | bytes accessed | tf_op | source)
XLA Modules:
  0.0 594.5 jit_solution(3427714757665129070)
XLA Ops:
  7.2 0.0 all-gather.2.cloned.1.call-start
  7.2 1.2 multiply_reduce_fusion.2
  8.5 1.9 fusion.7
  10.4 0.0 all-gather.2.cloned.1.call-update
  10.4 0.0 reduce-scatter.3.cloned.1.call-start
  11.7 0.0 copy-done.1
  11.8 0.1 multiply_reduce_fusion.3
  11.9 0.1 fusion.6
  12.0 76.1 %all-gather.2.cloned.1.call-done = bf16[4096,1152]{1,0:T(8,128)(2,1)} async-done(((bf16[128,1152]{1,0:T(8,128)(2,1)}), bf16[4096,1152]{1,0:T(8,128)(2,1)}) %all-gather.2.cloned.1.call-update) | async-done | bytes 9437200 | tf_op jit(solution)/shard_map/all_gather | solution.py:49
  88.1 7.6 %fusion.4 = (f32[128]{0:T(128)S(1)}, f32[128,4096]{1,0:T(8,128)S(1)}) fusion(f32[]{:T(128)} %bitcast.15, bf16[128,1152]{1,0:T(8,128)(2,1)S(1)} %fusion.6, bf16[4096,1152]{1,0:T(8,128)(2,1)} %all-gather.2.cloned.1.call-done, f32[]{:T(128)} %bitcast.10, s32[128]{0:T(128)S(1)} %iota_add_fusion), kind=kOutput, calls=%fused_computation.9 | convolution fusion | flops 1214775168 | bytes 11830280 | tf_op jit(solution)/shard_map/dot_general | solution.py:54
  95.7 8.1 %fusion.9 = f32[4096,1152]{1,0:T(8,128)} fusion(bf16[128,1152]{1,0:T(8,128)(2,1)S(1)} %fusion.6, f32[128,4096]{1,0:T(8,128)S(1)} %get-tuple-element.4, s32[128]{0:T(128)S(1)} %iota_add_fusion), kind=kOutput, calls=%fused_computation.30 | convolution fusion | flops 1212153856 | bytes 21266944 | tf_op jit(solution)/shard_map/dot_general | solution.py:28
  103.8 0.0 reduce-scatter.3.cloned.1.call-update
  103.8 0.0 reduce-scatter.5.cloned.1.call-start
  103.9 2.5 collective-permute-start
  106.4 303.5 %collective-permute-done = bf16[4096,1152]{1,0:T(8,128)(2,1)S(1)} collective-permute-done((bf16[4096,1152]{1,0:T(8,128)(2,1)}, bf16[4096,1152]{1,0:T(8,128)(2,1)S(1)}, u32[]{:S(2)}, u32[]{:S(2)}) %collective-permute-start) | collective-permute-done | bytes 9437216 | tf_op jit(solution)/shard_map/ppermute | solution.py:15
  409.9 3.7 fusion.5
  413.7 1.3 copy-done.2
  415.0 7.9 %fusion.8 = f32[4096,1152]{1,0:T(8,128)} fusion(bf16[128,1152]{1,0:T(8,128)(2,1)S(1)} %fusion.6, f32[128,4096]{1,0:T(8,128)S(1)} %get-tuple-element.6), kind=kOutput, calls=%fused_computation.29 | convolution fusion | flops 1210056704 | bytes 21266432 | tf_op jit(solution)/shard_map/dot_general | solution.py:28
  422.9 0.0 reduce-scatter.5.cloned.1.call-update
  422.9 6.3 %fusion.10 = f32[128,1152]{1,0:T(8,128)} fusion(bf16[4096,1152]{1,0:T(8,128)(2,1)} %all-gather.2.cloned.1.call-done, f32[128,4096]{1,0:T(8,128)S(1)} %get-tuple-element.4, s32[128]{0:T(128)S(1)} %iota_add_fusion), kind=kOutput, calls=%fused_computation.31 | convolution fusion | flops 1212153856 | bytes 12124672 | tf_op jit(solution)/shard_map/dot_general | solution.py:60
  429.2 0.4 collective-permute-start.1
  429.6 6.3 %multiply_reduce_fusion.1 = (f32[128]{0:T(128)S(1)}, f32[128,1152]{1,0:T(8,128)S(1)}) fusion(f32[128,1152]{1,0:T(8,128)S(1)} %copy-done.1, f32[128]{0:T(128)S(1)} %add_sqrt_fusion.1, f32[128,1152]{1,0:T(8,128)} %fusion.10, bf16[4096,1152]{1,0:T(8,128)(2,1)} %copy-done.3, f32[128,4096]{1,0:T(8,128)} %copy-done.2, f32[]{:T(128)} %bitcast.11), kind=kOutput, calls=%fused_computation.18 | convolution fusion | flops 1210793856 | bytes 13304836 | tf_op jit(solution)/shard_map/dot_general | solution.py:60
  435.9 0.0 copy-start
  436.0 30.8 %collective-permute-done.1 = f32[128,1152]{1,0:T(8,128)S(1)} collective-permute-done((f32[128,1152]{1,0:T(8,128)}, f32[128,1152]{1,0:T(8,128)S(1)}, u32[]{:S(2)}, u32[]{:S(2)}) %collective-permute-start.1) | collective-permute-done | bytes 589856 | tf_op jit(solution)/shard_map/ppermute | solution.py:15
  466.7 97.5 %reduce-scatter.5.cloned.1.call-done = f32[128,1152]{1,0:T(8,128)} async-done(((f32[4096,1152]{1,0:T(8,128)}), f32[128,1152]{1,0:T(8,128)}) %reduce-scatter.5.cloned.1.call-update) | async-done | bytes 589840 | tf_op jit(solution)/shard_map/reduce_scatter | solution.py:62
  564.3 1.1 add.75
  565.4 10.6 %collective-permute-start.2 = (f32[128,1152]{1,0:T(8,128)S(1)}, f32[128,1152]{1,0:T(8,128)S(1)}, u32[]{:S(2)}, u32[]{:S(2)}) collective-permute-start(f32[128,1152]{1,0:T(8,128)S(1)} %add.75), channel_id=1, source_target_pairs={{0,224},{32,0},{64,32},{96,64},{128,96},{160,128},{192,160},{224,1... | collective-permute-start | bytes 1769480 | tf_op jit(solution)/shard_map/ppermute | solution.py:15
  576.0 0.5 add_multiply_fusion
  576.5 1.0 subtract_divide_fusion.1
  577.5 9.3 %collective-permute-done.2 = f32[128,1152]{1,0:T(8,128)S(1)} collective-permute-done((f32[128,1152]{1,0:T(8,128)S(1)}, f32[128,1152]{1,0:T(8,128)S(1)}, u32[]{:S(2)}, u32[]{:S(2)}) %collective-permute-start.2) | collective-permute-done | bytes 589856 | tf_op jit(solution)/shard_map/ppermute | solution.py:15
  586.7 0.2 multiply_reduce_fusion
  587.0 1.0 subtract_divide_fusion
  (9 shorter events, 0.0 us)
Async XLA Ops:
  7.2 4.6 copy-start.1
  7.2 81.0 %all-gather.2.cloned.1.call-start = ((), (), s32[]{:S(2)}) async-start(), calls=%async_computation.2 | async-start | bytes 9732096 | tf_op jit(solution)/shard_map/all_gather | solution.py:49
  10.4 418.8 %reduce-scatter.3.cloned.1.call-start = ((), (), s32[]{:S(2)}) async-start(), calls=%async_computation.3 | async-start | bytes 19464192 | tf_op jit(solution)/shard_map/reduce_scatter | solution.py:62
  103.8 460.5 %reduce-scatter.5.cloned.1.call-start = ((), (), s32[]{:S(2)}) async-start(), calls=%async_computation.4 | async-start | bytes 19464192 | tf_op jit(solution)/shard_map/reduce_scatter | solution.py:62
  103.9 306.1 %collective-permute-start = (bf16[4096,1152]{1,0:T(8,128)(2,1)}, bf16[4096,1152]{1,0:T(8,128)(2,1)S(1)}, u32[]{:S(2)}, u32[]{:S(2)}) collective-permute-start(bf16[4096,1152]{1,0:T(8,128)(2,1)} %all-gather.2.cloned.1.call-done), channel_id=1, source_target_pairs={{0,32},{32,64},{64,96},{96,128},{128,160},{160,192},{192,224},{224... | collective-permute-start | bytes 28311560 | tf_op jit(solution)/shard_map/ppermute | solution.py:15
  409.9 3.7 copy-start.3
  413.7 1.3 copy-start.2
  429.2 37.5 %collective-permute-start.1 = (f32[128,1152]{1,0:T(8,128)}, f32[128,1152]{1,0:T(8,128)S(1)}, u32[]{:S(2)}, u32[]{:S(2)}) collective-permute-start(f32[128,1152]{1,0:T(8,128)} %reduce-scatter.3.cloned.1.call-done), channel_id=1, source_target_pairs={{0,32},{32,64},{64,96},{96,128},{128,160},{160,192},{192,224},{224... | collective-permute-start | bytes 1769480 | tf_op jit(solution)/shard_map/ppermute | solution.py:15
  435.9 150.8 %copy-start = (f32[128,1152]{1,0:T(8,128)S(1)}, f32[128,1152]{1,0:T(8,128)}, u32[]{:S(2)}) copy-start(f32[128,1152]{1,0:T(8,128)} %param.5) | copy-start | bytes 1769476
  565.4 21.3 %collective-permute-start.2 = (f32[128,1152]{1,0:T(8,128)S(1)}, f32[128,1152]{1,0:T(8,128)S(1)}, u32[]{:S(2)}, u32[]{:S(2)}) collective-permute-start(f32[128,1152]{1,0:T(8,128)S(1)} %add.75), channel_id=1, source_target_pairs={{0,224},{32,0},{64,32},{96,64},{128,96},{160,128},{192,160},{224,1... | collective-permute-start | bytes 1769480 | tf_op jit(solution)/shard_map/ppermute | solution.py:15
Sparse Core Ops, SparseCore 0:
  10.5 77.5 all-gather.1
  103.9 147.0 reduce-scatter.2
  423.0 141.2 reduce-scatter.4
where the time goes:
time: 598 us; the launch traced here: 595 us
  waiting for transfers between devices  517 us (86%)
  matrix products  40 us (7%)
  between operations  15.1 us (3%)
  starting transfers between devices  13.6 us (2%)
  other arithmetic  7.24 us (1%)
    ppermute x3, waiting for transfers between devices, from_behind(): return lax.ppermute(value, axis, pairs)  344 us
    reduce_scatter x2, waiting for transfers between devices, on_device(): lax.psum_scatter(partial_sum, 'ing', scatter_dimension=0, tiled=True)  97.5 us
    all_gather x1, waiting for transfers between devices, on_device(): text_block = lax.all_gather(text_low, 'ing', axis=0, tiled=True)  76.1 us
    dot_general x2, matrix products, first_contract(): lax.dot_general(left_side, right_side, (((0,), (0,)), ((), ())), preferre...  16 us
    ppermute x3, starting transfers between devices, from_behind(): return lax.ppermute(value, axis, pairs)  13.5 us
    dot_general x2, matrix products, on_device(): jnp.dot(coefficient, text_block, preferred_element_type=jnp.float32)  12.7 us
  transfers between devices with their start and end apart: 6, of which 5 were waited for; matrix products, arithmetic and copies ran while one was open for 4% of the time, Pallas kernels for 0%

commit v1 on v0

v1 whole, which is shorter than its diff:
```python
import functools

import jax
import jax.numpy as jnp
from jax import lax
from jax.experimental import pallas as pl
from jax.experimental.pallas import tpu as pltpu
from jax.sharding import PartitionSpec as P

STEPS = 2
EPSILON = 1e-06
MESH = pl.DeviceIdType.MESH
F32, BF16 = jnp.float32, jnp.bfloat16

CORES, RING = 2, 8
N_AG = 4
N_RS = 2
N_T = 2


def column_dot(left, right):
    return lax.dot_general(left, right, (((1,), (1,)), ((), ())), preferred_element_type=F32)


def kernel(
    image_ref, text_ref, scale_ref, bias_ref,
    loss_ref, image_grad_ref, text_grad_ref,
    img, txt, coef, coef_t, part, tgrad, racc, sacc, rloss, sloss, losses,
    sib_out, sib_in, yp_out, yp_in, back_out, back_in,
    unit_i, unit_t, norm_i, norm_t,
    ag_s, ag_r, t_s, t_r, f_s, rs_s, rs_r, l_s, l_r, sib_s, sib_r, yp_s, yp_r, bk_s, bk_r,
):
    rows, embed = image_ref.shape
    n_grp = lax.axis_size("grp")
    g, i = lax.axis_index("grp"), lax.axis_index("ing")
    core, z, y = i % CORES, (i // CORES) % RING, i // (CORES * RING)
    dz = 1 - 2 * core

    def device(group, y_, z_, core_):
        return (group, (y_ * RING + z_) * CORES + core_)

    nxt = device(g, y, lax.rem(z + dz + RING, RING), core)
    prv = device(g, y, lax.rem(z - dz + RING, RING), core)
    sib = device(g, y, z, 1 - core)
    ypart = device(g, 1 - y, z, core)
    ahead = device(lax.rem(g + 1, n_grp), 1 - y, z, core)
    behind = device(lax.rem(g + n_grp - 1, n_grp), 1 - y, z, core)

    barrier = pltpu.get_barrier_semaphore()
    for peer in (nxt, prv, sib, ypart, ahead, behind):
        pl.semaphore_signal(barrier, inc=1, device_id=peer, device_id_type=MESH)

    def send(src, dst, s_sem, r_sem, to):
        copy = pltpu.make_async_remote_copy(
            src_ref=src, dst_ref=dst, send_sem=s_sem, recv_sem=r_sem,
            device_id=to, device_id_type=MESH,
        )
        copy.start()
        sent.append(copy)

    def landed(dst, r_sem):
        pltpu.make_async_remote_copy(
            src_ref=dst, dst_ref=dst, send_sem=r_sem, recv_sem=r_sem,
            device_id=nxt, device_id_type=MESH,
        ).wait_recv()

    sent = []

    def normalize(raw_ref, unit, norm, low):
        raw = raw_ref[...]
        norms = jnp.sqrt(jnp.sum(raw * raw, axis=1, keepdims=True) + EPSILON)
        units = raw / norms
        unit[...] = units
        norm[...] = norms
        low[...] = units.astype(BF16)

    def img_rows(slot, c):
        n = rows // N_AG
        return img.at[pl.ds(slot * rows + c * n, n)]

    def ring_on(slot):
        for c in range(N_AG):
            if slot < RING - 1:
                landed(img_rows(slot, c), ag_r.at[slot, c])
            to = (slot + 1) % RING
            if to < RING - 1:
                send(img_rows(slot, c), img_rows(to, c), ag_s.at[to, c], ag_r.at[to, c], nxt)

    def t_rows(slot, c):
        n = rows // N_T
        return txt.at[pl.ds(slot * rows + c * n, n)]

    def t_send(slot, c, to_slot, sem, to):
        send(t_rows(slot, c), t_rows(to_slot, c), f_s.at[sem, c], t_r.at[to_slot, c], to)

    def t_landed(slot, c):
        landed(t_rows(slot, c), t_r.at[slot, c])

    normalize(image_ref, unit_i, norm_i, img.at[pl.ds((RING - 1) * rows, rows)])
    pl.semaphore_wait(barrier, 6)
    ring_on(RING - 1)
    normalize(text_ref, unit_t, norm_t, txt.at[pl.ds(0, rows)])
    for c in range(N_T):
        t_send(0, c, 2, 0, ahead)
        t_send(0, c, 1, 1, ypart)
        t_send(0, c, 4, 2, sib)

    ring_on(0)
    for c in range(N_T):
        t_landed(1, c)
        if c == 0:
            t_send(1, c, 3, 3, ahead)
        t_send(1, c, 5, 4, sib)
        t_landed(2, c)
        if c == 1:
            t_send(2, c, 3, 3, ypart)
        t_send(2, c, 6, 5, sib)
    ring_on(1)
    ring_on(2)
    for c in range(N_T):
        t_landed(3, c)
        t_send(3, c, 7, 6, sib)
    ring_on(3)
    for slot in range(4, 8):
        for c in range(N_T):
            t_landed(slot, c)

    scale, bias = scale_ref[0], bias_ref[0]
    wide = 2 * rows
    blocks = 8 * rows // wide
    apart = lax.broadcasted_iota(jnp.int32, (wide, wide), 1) - lax.broadcasted_iota(
        jnp.int32, (wide, wide), 0
    )

    def score(u):
        def block(b, total):
            at = pl.ds(pl.multiple_of(b * wide, wide), wide)
            x = scale * column_dot(txt[at, :], img[pl.ds(u * wide, wide), :]) + bias
            own = apart == (7 * rows - u * wide) + b * wide
            m = jnp.where(own, -x, x)
            e = jnp.exp(-jnp.abs(m))
            one = 1.0 + e
            inv = 1.0 / one
            log1p = jnp.log(one) + (e - (one - 1.0)) * inv
            total = total + jnp.sum(jnp.maximum(m, 0.0) + log1p, axis=0, keepdims=True)
            sig = jnp.where(m >= 0.0, inv, e * inv)
            cf = jnp.where(own, -sig, sig).astype(BF16)
            coef[at, :] = cf
            coef_t[:, at] = cf.T
            return total

        losses[:, pl.ds(u * wide, wide)] = lax.fori_loop(
            0, blocks, block, jnp.zeros((1, wide), F32)
        )

    def image_part(u):
        step = 3 * 128

        def tile(n, carry):
            at = pl.ds(pl.multiple_of(n * step, step), step)
            part[pl.ds(u * wide, wide), at] = jnp.dot(
                coef_t[...], txt[:, at], preferred_element_type=F32
            )
            return carry

        lax.fori_loop(0, embed // step, tile, 0)

    def text_part(u):
        def block(b, carry):
            at = pl.ds(pl.multiple_of(b * wide, wide), wide)
            add = jnp.dot(coef[at, :], img[pl.ds(u * wide, wide), :], preferred_element_type=F32)
            tgrad[at, :] = add if u == 0 else tgrad[at, :] + add
            return carry

        lax.fori_loop(0, blocks, block, 0)

    def sum_on(slot):
        mine = losses[:, pl.ds(slot * rows, rows)]
        if slot > 0:
            landed(rloss.at[slot - 1], l_r.at[slot - 1])
            mine = mine + rloss[slot - 1, 0:1, :]
        sloss[slot] = jnp.broadcast_to(mine, (8, rows))
        send(sloss.at[slot], rloss.at[slot], l_s.at[slot], l_r.at[slot], nxt)
        n = rows // N_RS
        for c in range(N_RS):
            at = pl.ds(c * n, n)
            value = part[pl.ds(slot * rows + c * n, n), :]
            if slot > 0:
                landed(racc.at[slot - 1, at], rs_r.at[slot - 1, c])
                value = value + racc[slot - 1, at, :].astype(F32)
            sacc[slot, at, :] = value.astype(BF16)
            send(sacc.at[slot, at], racc.at[slot, at], rs_s.at[slot, c], rs_r.at[slot, c], nxt)

    def shard(slot):
        return pl.ds(slot * rows, rows)

    score(0)
    image_part(0)
    sum_on(0)
    text_part(0)
    ring_on(4)
    score(1)
    image_part(1)
    sum_on(1)
    text_part(1)
    ring_on(5)
    score(2)
    image_part(2)
    sum_on(2)
    text_part(2)
    ring_on(6)
    score(3)
    text_part(3)
    for s in (2, 3, 0, 1):
        sib_out[s] = tgrad[shard(4 + s), :].astype(BF16)
        send(sib_out.at[s], sib_in.at[s], sib_s.at[s], sib_r.at[s], sib)
    sum_on(3)
    image_part(3)

    def from_sib(s):
        landed(sib_in.at[s], sib_r.at[s])
        tgrad[shard(s), :] = tgrad[shard(s), :] + sib_in[s].astype(F32)

    def to_partner(s, n):
        from_sib(s)
        yp_out[n] = tgrad[shard(s), :].astype(BF16)
        send(yp_out.at[n], yp_in.at[n], yp_s.at[n], yp_r.at[n], ypart)

    to_partner(3, 0)
    to_partner(1, 1)
    from_sib(2)
    from_sib(0)
    sum_on(4)
    landed(yp_in.at[0], yp_r.at[0])
    back_out[...] = (tgrad[shard(2), :] + yp_in[0].astype(F32)).astype(BF16)
    send(back_out, back_in, bk_s, bk_r, behind)
    sum_on(5)
    landed(yp_in.at[1], yp_r.at[1])
    tgrad[shard(0), :] = tgrad[shard(0), :] + yp_in[1].astype(F32)

    def restore(unit_grad, unit, norm):
        units = unit[...]
        return (unit_grad - units * jnp.sum(units * unit_grad, axis=1, keepdims=True)) / norm[...]

    sum_on(6)
    landed(back_in, bk_r)
    text_grad_ref[...] = restore(
        scale * (tgrad[shard(0), :] + back_in[...].astype(F32)), unit_t, norm_t
    )

    landed(rloss.at[6], l_r.at[6])
    n_scored = STEPS * rows * lax.axis_size("ing")
    loss_ref[...] = (losses[:, shard(7)] + rloss[6, 0:1, :]) / n_scored
    n = rows // N_RS
    for c in range(N_RS):
        landed(racc.at[6, pl.ds(c * n, n)], rs_r.at[6, c])
    image_grad_ref[...] = restore(
        scale * (part[shard(7), :] + racc[6].astype(F32)), unit_i, norm_i
    )
    for copy in sent:
        copy.wait_send()


def on_device(image_emb, text_emb, logit_scale, logit_bias):
    rows, embed = image_emb.shape
    full, dma = RING * rows, pltpu.SemaphoreType.DMA
    wide = 2 * rows
    vmem, smem = pl.BlockSpec(memory_space=pltpu.VMEM), pl.BlockSpec(memory_space=pltpu.SMEM)
    loss, image_grad, text_grad = pl.pallas_call(
        kernel,
        out_shape=(
            jax.ShapeDtypeStruct((1, rows), F32),
            jax.ShapeDtypeStruct((rows, embed), F32),
            jax.ShapeDtypeStruct((rows, embed), F32),
        ),
        in_specs=[vmem, vmem, smem, smem],
        out_specs=(vmem, vmem, vmem),
        scratch_shapes=[
            pltpu.VMEM((full, embed), BF16),
            pltpu.VMEM((full, embed), BF16),
            pltpu.VMEM((full, wide), BF16),
            pltpu.VMEM((wide, full), BF16),
            pltpu.VMEM((full, embed), F32),
            pltpu.VMEM((full, embed), F32),
            pltpu.VMEM((7, rows, embed), BF16),
            pltpu.VMEM((7, rows, embed), BF16),
            pltpu.VMEM((7, 8, rows), F32),
            pltpu.VMEM((7, 8, rows), F32),
            pltpu.VMEM((1, full), F32),
            pltpu.VMEM((4, rows, embed), BF16),
            pltpu.VMEM((4, rows, embed), BF16),
            pltpu.VMEM((2, rows, embed), BF16),
            pltpu.VMEM((2, rows, embed), BF16),
            pltpu.VMEM((rows, embed), BF16),
            pltpu.VMEM((rows, embed), BF16),
            pltpu.VMEM((rows, embed), F32),
            pltpu.VMEM((rows, embed), F32),
            pltpu.VMEM((rows, 1), F32),
            pltpu.VMEM((rows, 1), F32),
            dma((7, N_AG)), dma((7, N_AG)),
            dma((8, N_T)), dma((8, N_T)), dma((7, N_T)),
            dma((7, N_RS)), dma((7, N_RS)),
            dma((7,)), dma((7,)),
            dma((4,)), dma((4,)),
            dma((2,)), dma((2,)),
            dma, dma,
        ],
        compiler_params=pltpu.CompilerParams(
            collective_id=0, has_side_effects=True, vmem_limit_bytes=56 * 2**20
        ),
        cost_estimate=pl.CostEstimate(
            flops=6 * full * full * embed, bytes_accessed=16 * rows * embed, transcendentals=3 * full * full
        ),
    )(image_emb, text_emb, logit_scale, logit_bias)
    return loss.reshape(rows), image_grad, text_grad


def solution(mesh):
    placed = (P(("grp", "ing"), None), P(("grp", "ing"), None), P(), P())
    return jax.shard_map(
        on_device,
        mesh=mesh,
        in_specs=placed,
        out_specs=(P(("grp", "ing")), P(("grp", "ing"), None), P(("grp", "ing"), None)),
        check_vma=False,
    )
```

time: 598 us -> 83.4 us (0.14)
  waiting for transfers between devices: 517 us -> 0 us
  Pallas kernels: 0 us -> 77.4 us
  matrix products: 40 us -> 0 us
  starting transfers between devices: 13.6 us -> 0 us
  between operations: 15.1 us -> 1.94 us
  other arithmetic: 7.24 us -> 0 us
    ppermute x3 -> x0, waiting for transfers between devices: 344 us -> none  [from_behind(): return lax.ppermute(value, axis, pairs)]
    reduce_scatter x2 -> x0, waiting for transfers between devices: 97.5 us -> none  [on_device(): lax.psum_scatter(partial_sum, 'ing', scatter_dimension=0, tiled=True)]
    pallas_call x0 -> x1, Pallas kernels: none -> 77.4 us  [on_device(): pl.pallas_call(kernel, out_shape=(jax.ShapeDtypeStruct((1, rows), F32), j...]
    all_gather x1 -> x0, waiting for transfers between devices: 76.1 us -> none  [on_device(): text_block = lax.all_gather(text_low, 'ing', axis=0, tiled=True)]
    dot_general x6 -> x0, matrix products: 40 us -> none  [the longest x2 16 us: first_contract(): lax.dot_general(left_side, right_side, (((0,), (0,)), ((), ())), preferre...]
    ppermute x3 -> x0, starting transfers between devices: 13.5 us -> none  [from_behind(): return lax.ppermute(value, axis, pairs)]
  transfers between devices with their start and end apart: 6 -> 0, of which waited for: 5 -> 0; matrix products, arithmetic and copies ran while one was open for 4% -> 0% of each run, Pallas kernels for 0% -> 0%
where the time goes in v1:
time: 83.4 us; the launch traced here: 83.3 us
  Pallas kernels  77.4 us (93%)
  local copies, waits for them, and re-layouts  3.92 us (5%)
  between operations  1.94 us (2%)
    pallas_call x1, Pallas kernels, on_device(): pl.pallas_call(kernel, out_shape=(jax.ShapeDtypeStruct((1, rows), F32), j...  77.4 us
    unnamed x7, local copies, waits for them, and re-layouts  3.92 us

profile of v1, /device:TPU:1, one launch (start us, length us, event | category | flops | bytes accessed | tf_op | source)
XLA Modules:
  0.0 83.3 jit_solution(9854475177585595365)
XLA Ops:
  1.9 77.4 %shard_map.67 = (f32[1,128]{1,0:T(1,128)}, f32[128,1152]{1,0:T(8,128)}, f32[128,1152]{1,0:T(8,128)}) custom-call(f32[128,1152]{1,0:T(8,128)} %image_ref.1, f32[128,1152]{1,0:T(8,128)} %text_ref.1, f32[1]{0:T(128)S(6)} %copy.10.scale_ref, f32[1]{0:T(128)S(6)} %copy.11.bias_ref), custom_call_target="tpu_custom_call" | custom-call | flops 7247757312 | bytes 2359296 | tf_op jit(solution)/shard_map/pallas_call | solution.py:269
  79.3 0.0 copy-start.1
  79.4 0.6 copy-done.1
  80.0 0.5 copy.12
  80.5 0.0 copy-start
  80.5 2.0 %copy.13 = f32[128,1152]{1,0:T(8,128)} copy(f32[128,1152]{1,0:T(8,128)} %get-tuple-element.13) | data formatting | bytes 1179648
  82.5 0.0 copy-done
  82.5 0.8 copy.14
Async XLA Ops:
  79.3 0.6 copy-start.1
  80.5 2.0 %copy-start = (f32[128,1152]{1,0:T(8,128)S(1)}, f32[128,1152]{1,0:T(8,128)}, u32[]{:S(2)}) copy-start(f32[128,1152]{1,0:T(8,128)} %get-tuple-element.14) | copy-start | bytes 1769476

commit v2 on v0

v2 whole, which is shorter than its diff:
```python
import jax
import jax.numpy as jnp
from jax import lax
from jax.experimental import pallas as pl
from jax.experimental.pallas import tpu as pltpu
from jax.sharding import PartitionSpec as P

STEPS = 2
EPSILON = 1e-06
MESH = pl.DeviceIdType.MESH
F32, BF16 = jnp.float32, jnp.bfloat16

CORES, RING = 2, 8
N_AG = 2
N_RS = 4
N_T = 4
SLOT = {1: 0, 7: 1, 2: 2, 6: 3, 3: 4, 5: 5, 4: 6, 0: 7}
TURN = 4
LANDS = {hop: n for n, hop in enumerate([*range(TURN + 1, RING + 1), *range(TURN - 1)])}


def column_dot(left, right):
    return lax.dot_general(left, right, (((1,), (1,)), ((), ())), preferred_element_type=F32)


def row_norms(raw):
    return jnp.sqrt(jnp.sum(raw * raw, axis=1, keepdims=True) + EPSILON)


def kernel(
    image_ref, text_ref, scale_ref, bias_ref,
    loss_ref, image_sum_ref, text_sum_ref,
    raw_i, raw_t, img, txt, coef, part, tgrad, racc, sacc, rloss, sloss, losses,
    sib_out, sib_in, d_out, d_in,
    in_sem, ag_s, ag_r, t_r, f_s, rs_s, rs_r, l_s, l_r, sib_s, sib_r, d_s, d_r,
):
    rows, embed = raw_i.shape
    n_grp = lax.axis_size("grp")
    g, i = lax.axis_index("grp"), lax.axis_index("ing")
    core, z, y = i % CORES, (i // CORES) % RING, i // (CORES * RING)
    dz = 1 - 2 * core

    def device(group, y_, z_, core_):
        return (group, (y_ * RING + z_) * CORES + core_)

    nxt = device(g, y, lax.rem(z + dz + RING, RING), core)
    prv = device(g, y, lax.rem(z - dz + RING, RING), core)
    sib = device(g, y, z, 1 - core)
    ypart = device(g, 1 - y, z, core)
    ahead = device(lax.rem(g + 1, n_grp), 1 - y, z, core)
    behind = device(lax.rem(g + n_grp - 1, n_grp), 1 - y, z, core)

    barrier = pltpu.get_barrier_semaphore()
    for peer in (nxt, prv, sib, ypart, ahead, behind):
        pl.semaphore_signal(barrier, inc=1, device_id=peer, device_id_type=MESH)
    fetch_i = pltpu.make_async_copy(image_ref, raw_i, in_sem.at[0])
    fetch_t = pltpu.make_async_copy(text_ref, raw_t, in_sem.at[1])
    fetch_i.start()
    fetch_t.start()

    sent = []

    def send(src, dst, s_sem, r_sem, to):
        copy = pltpu.make_async_remote_copy(
            src_ref=src, dst_ref=dst, send_sem=s_sem, recv_sem=r_sem,
            device_id=to, device_id_type=MESH,
        )
        copy.start()
        sent.append(copy)

    def landed(dst, sem):
        pltpu.make_async_remote_copy(
            src_ref=dst, dst_ref=dst, send_sem=sem, recv_sem=sem,
            device_id=nxt, device_id_type=MESH,
        ).wait_recv()

    def img_rows(hop, c):
        n = rows // N_AG
        return img.at[pl.ds(SLOT[hop] * rows + c * n, n)]

    def ring_send(hop, to, c, peer):
        send(img_rows(hop, c), img_rows(to, c), ag_s.at[to - 1, c], ag_r.at[to - 1, c], peer)

    def ring_chunk(hop, c):
        landed(img_rows(hop, c), ag_r.at[hop - 1, c])
        if hop < RING // 2:
            ring_send(hop, hop + 1, c, nxt)
        elif hop > RING // 2 + 1:
            ring_send(hop, hop - 1, c, prv)

    def t_rows(slot, c):
        n = rows // N_T
        return txt.at[pl.ds(slot * rows + c * n, n)]

    def t_send(slot, c, to_slot, sem, to):
        send(t_rows(slot, c), t_rows(to_slot, c), f_s.at[sem, c], t_r.at[to_slot, c], to)

    def t_landed(slot, c):
        landed(t_rows(slot, c), t_r.at[slot, c])

    def normalize(raw_ref, low):
        raw = raw_ref[...]
        low[...] = (raw / row_norms(raw)).astype(BF16)

    scale, bias = scale_ref[0], bias_ref[0]
    wide = 2 * rows

    def images(u):
        return pl.ds(u * wide, wide)

    def score(u):
        dots = column_dot(txt[...], img[images(u), :])
        x = scale * dots + bias
        e = jnp.exp(x)
        one = 1.0 + e
        inv = pl.reciprocal(one, approx=True)
        inv = inv * (2.0 - one * inv)
        loss = jnp.log(one) + (e - (one - 1.0)) * inv
        coef[u] = (e * inv).astype(BF16)
        losses[:, images(u)] = jnp.sum(loss, axis=0, keepdims=True)
        if u == 3:
            x = x[:rows, rows:]
            own = lax.broadcasted_iota(jnp.int32, x.shape, 0) == lax.broadcasted_iota(
                jnp.int32, x.shape, 1
            )
            m = jnp.exp(-jnp.abs(x))
            one_m = 1.0 + m
            pair = jnp.log(one_m) + (m - (one_m - 1.0)) / one_m + jnp.maximum(-x, 0.0)
            inv = inv[:rows, rows:]
            coef[u, :rows, rows:] = jnp.where(own, -inv, e[:rows, rows:] * inv).astype(BF16)
            loss = jnp.concatenate(
                [jnp.where(own, pair, loss[:rows, rows:]), loss[rows:, rows:]], axis=0
            )
            losses[:, pl.ds(7 * rows, rows)] = jnp.sum(loss, axis=0, keepdims=True)

    def image_part(u):
        part[images(u), :] = lax.dot_general(
            coef[u], txt[...], (((0,), (0,)), ((), ())), preferred_element_type=F32
        )

    def text_part(u, first):
        add = jnp.dot(coef[u], img[images(u), :], preferred_element_type=F32)
        tgrad[...] = add if first else tgrad[...] + add

    def sum_on(hop, c):
        slot = SLOT[hop]
        to, peer = (hop + 1, nxt) if hop >= TURN else (hop - 1, prv)
        into, came = LANDS[to], LANDS.get(hop)
        n = rows // N_RS
        at = pl.ds(c * n, n)
        value = part[pl.ds(slot * rows + c * n, n), :]
        if came is not None:
            landed(racc.at[came, at], rs_r.at[came, c])
            value = value + racc[came, at, :].astype(F32)
        sacc[slot, at, :] = value.astype(BF16)
        send(sacc.at[slot, at], racc.at[into, at], rs_s.at[slot, c], rs_r.at[into, c], peer)
        if c == 0:
            mine = losses[:, pl.ds(slot * rows, rows)]
            if came is not None:
                landed(rloss.at[came], l_r.at[came])
                mine = mine + rloss[came, 0:1, :]
            sloss[slot] = jnp.broadcast_to(mine, (8, rows))
            send(sloss.at[slot], rloss.at[into], l_s.at[slot], l_r.at[into], peer)

    def sums_on(hop):
        for c in range(N_RS):
            sum_on(hop, c)

    half = rows // 2

    def to_sib(s):
        sib_out[s] = tgrad[pl.ds((4 + s) * rows, rows), :].astype(BF16)
        send(sib_out.at[s], sib_in.at[s], sib_s.at[s], sib_r.at[s], sib)

    def from_sib(s):
        landed(sib_in.at[s], sib_r.at[s])
        at = pl.ds(s * rows, rows)
        tgrad[at, :] = tgrad[at, :] + sib_in[s].astype(F32)

    def t_half(s, h):
        return pl.ds(s * rows + h * half, half)

    def d_send(m, s, h, to):
        d_out[m] = tgrad[t_half(s, h), :].astype(BF16)
        send(d_out.at[m], d_in.at[m], d_s.at[m], d_r.at[m], to)

    def d_add(m, s, h):
        landed(d_in.at[m], d_r.at[m])
        at = t_half(s, h)
        tgrad[at, :] = tgrad[at, :] + d_in[m].astype(F32)

    fetch_i.wait()
    normalize(raw_i, img.at[pl.ds((RING - 1) * rows, rows)])
    pl.semaphore_wait(barrier, 6)
    for c in range(N_AG):
        ring_send(0, 1, c, nxt)
        ring_send(0, 7, c, prv)
    fetch_t.wait()
    normalize(raw_t, txt.at[pl.ds(0, rows)])
    for c in range(N_T):
        t_send(0, c, 1, 1, ypart)
        t_send(0, (c + 2) % N_T, 2, 0, ahead)
    for c in range(N_T):
        t_send(0, c, 4, 2, sib)

    def ring_on(hop, back, c):
        ring_chunk(hop, c)
        ring_chunk(back, c)

    def partner_text(c):
        t_landed(1, c)
        if c < 2:
            t_send(1, c, 3, 3, ahead)
        t_send(1, c, 5, 4, sib)

    def behind_text(c):
        t_landed(2, c)
        if c >= 2:
            t_send(2, c, 3, 3, ypart)
        t_send(2, c, 6, 5, sib)

    def far_text(c):
        t_landed(3, c)
        t_send(3, c, 7, 6, sib)

    partner_text(0)
    behind_text(2)
    partner_text(1)
    ring_on(1, 7, 0)
    behind_text(3)
    partner_text(2)
    behind_text(0)
    partner_text(3)
    ring_on(1, 7, 1)
    behind_text(1)
    far_text(2)
    far_text(0)
    far_text(3)
    ring_on(2, 6, 0)
    far_text(1)
    for slot in range(4, 8):
        for c in range(N_T):
            t_landed(slot, c)
    score(0)
    ring_on(2, 6, 1)
    score(1)
    image_part(1)
    ring_on(3, 5, 0)
    text_part(1, True)
    image_part(0)
    text_part(0, False)
    ring_on(3, 5, 1)
    score(2)
    image_part(2)
    sums_on(3)
    ring_chunk(4, 0)
    ring_chunk(4, 1)
    score(3)
    image_part(3)
    sums_on(4)
    text_part(2, False)
    text_part(3, False)
    for s in (3, 2, 1, 0):
        to_sib(s)
    sums_on(2)
    sums_on(5)
    from_sib(3)
    d_send(0, 3, 0, behind)
    d_send(1, 3, 1, ypart)
    from_sib(2)
    d_send(2, 2, 0, behind)
    from_sib(1)
    d_send(3, 1, 1, ypart)
    from_sib(0)
    sums_on(1)
    d_add(1, 2, 1)
    d_send(4, 2, 1, behind)
    sums_on(6)
    d_add(0, 1, 0)
    d_send(5, 1, 0, ypart)
    d_add(3, 0, 1)
    d_add(2, 0, 0)
    sums_on(7)
    d_add(5, 0, 0)
    d_add(4, 0, 1)
    text_sum_ref[...] = tgrad[pl.ds(0, rows), :]

    mine = losses[:, pl.ds(7 * rows, rows)]
    for came in (LANDS[0], LANDS[8]):
        landed(rloss.at[came], l_r.at[came])
        mine = mine + rloss[came, 0:1, :]
    loss_ref[...] = mine
    n = rows // N_RS
    for c in range(N_RS):
        at = pl.ds(c * n, n)
        value = part[pl.ds(7 * rows + c * n, n), :]
        for came in (LANDS[0], LANDS[8]):
            landed(racc.at[came, at], rs_r.at[came, c])
            value = value + racc[came, at, :].astype(F32)
        image_sum_ref[at, :] = value
    for copy in sent:
        copy.wait_send()


def finish(scored, image_ref, text_ref, image_sum_ref, text_sum_ref, loss_sum_ref, scale_ref,
           loss_ref, image_grad_ref, text_grad_ref):
    scale = scale_ref[0]

    def restore(raw_ref, sum_ref, out_ref):
        raw = raw_ref[...]
        norms = row_norms(raw)
        units = raw / norms
        grad = scale * sum_ref[...]
        out_ref[...] = (grad - units * jnp.sum(units * grad, axis=1, keepdims=True)) / norms

    restore(image_ref, image_sum_ref, image_grad_ref)
    restore(text_ref, text_sum_ref, text_grad_ref)

    @pl.when(pl.program_id(0) == 0)
    def _():
        loss_ref[...] = loss_sum_ref[0, :] / scored


def on_device(image_emb, text_emb, logit_scale, logit_bias):
    rows, embed = image_emb.shape
    full, dma = RING * rows, pltpu.SemaphoreType.DMA
    wide, half = 2 * rows, rows // 2
    whole, smem = pl.BlockSpec(memory_space=pltpu.VMEM), pl.BlockSpec(memory_space=pltpu.SMEM)
    far = pl.BlockSpec(memory_space=pl.ANY)
    vmem = pltpu.VMEM
    loss_sum, image_sum, text_sum = pl.pallas_call(
        kernel,
        out_shape=(
            jax.ShapeDtypeStruct((1, rows), F32),
            jax.ShapeDtypeStruct((rows, embed), F32),
            jax.ShapeDtypeStruct((rows, embed), F32),
        ),
        in_specs=[far, far, smem, smem],
        out_specs=(whole, whole, whole),
        scratch_shapes=[
            vmem((rows, embed), F32),
            vmem((rows, embed), F32),
            vmem((full, embed), BF16),
            vmem((full, embed), BF16),
            vmem((4, full, wide), BF16),
            vmem((full, embed), F32),
            vmem((full, embed), F32),
            vmem((7, rows, embed), BF16),
            vmem((7, rows, embed), BF16),
            vmem((7, 8, rows), F32),
            vmem((7, 8, rows), F32),
            vmem((1, full), F32),
            vmem((4, rows, embed), BF16),
            vmem((4, rows, embed), BF16),
            vmem((6, half, embed), BF16),
            vmem((6, half, embed), BF16),
            dma((2,)),
            dma((7, N_AG)), dma((7, N_AG)),
            dma((8, N_T)), dma((7, N_T)),
            dma((7, N_RS)), dma((7, N_RS)),
            dma((7,)), dma((7,)),
            dma((4,)), dma((4,)),
            dma((6,)), dma((6,)),
        ],
        compiler_params=pltpu.CompilerParams(
            collective_id=0, has_side_effects=True, vmem_limit_bytes=56 * 2**20
        ),
        cost_estimate=pl.CostEstimate(
            flops=6 * full * full * embed, bytes_accessed=16 * rows * embed, transcendentals=3 * full * full
        ),
    )(image_emb, text_emb, logit_scale, logit_bias)
    n_cut = 1
    tile = pl.BlockSpec((rows // n_cut, embed), lambda n: (n, 0))
    scored = STEPS * rows * lax.axis_size("ing")
    return pl.pallas_call(
        lambda *refs: finish(scored, *refs),
        grid=(n_cut,),
        out_shape=(
            jax.ShapeDtypeStruct((rows,), F32),
            jax.ShapeDtypeStruct((rows, embed), F32),
            jax.ShapeDtypeStruct((rows, embed), F32),
        ),
        in_specs=[tile, tile, tile, tile, pl.BlockSpec((1, rows), lambda n: (0, 0)), smem],
        out_specs=(pl.BlockSpec((rows,), lambda n: (0,)), tile, tile),
    )(image_emb, text_emb, image_sum, text_sum, loss_sum, logit_scale)


def solution(mesh):
    placed = (P(("grp", "ing"), None), P(("grp", "ing"), None), P(), P())
    return jax.shard_map(
        on_device,
        mesh=mesh,
        in_specs=placed,
        out_specs=(P(("grp", "ing")), P(("grp", "ing"), None), P(("grp", "ing"), None)),
        check_vma=False,
    )
```

time: 598 us -> 68.3 us (0.11)
  waiting for transfers between devices: 517 us -> 0 us
  Pallas kernels: 0 us -> 65.3 us
  matrix products: 40 us -> 0 us
  starting transfers between devices: 13.6 us -> 0 us
  between operations: 15.1 us -> 1.93 us
  other arithmetic: 7.24 us -> 0 us
    ppermute x3 -> x0, waiting for transfers between devices: 344 us -> none  [from_behind(): return lax.ppermute(value, axis, pairs)]
    reduce_scatter x2 -> x0, waiting for transfers between devices: 97.5 us -> none  [on_device(): lax.psum_scatter(partial_sum, 'ing', scatter_dimension=0, tiled=True)]
    all_gather x1 -> x0, waiting for transfers between devices: 76.1 us -> none  [on_device(): text_block = lax.all_gather(text_low, 'ing', axis=0, tiled=True)]
    pallas_call x0 -> x2, Pallas kernels: none -> 65.3 us  [the longest x1 62.3 us: on_device(): pl.pallas_call(kernel, out_shape=(jax.ShapeDtypeStruct((1, rows), F32), j...]
    dot_general x6 -> x0, matrix products: 40 us -> none  [the longest x2 16 us: first_contract(): lax.dot_general(left_side, right_side, (((0,), (0,)), ((), ())), preferre...]
    ppermute x3 -> x0, starting transfers between devices: 13.5 us -> none  [from_behind(): return lax.ppermute(value, axis, pairs)]
  transfers between devices with their start and end apart: 6 -> 0, of which waited for: 5 -> 0; matrix products, arithmetic and copies ran while one was open for 4% -> 0% of each run, Pallas kernels for 0% -> 0%
where the time goes in v2:
time: 68.3 us; the launch traced here: 67.2 us
  Pallas kernels  65.3 us (96%)
  between operations  1.93 us (3%)
    pallas_call x1, Pallas kernels, on_device(): pl.pallas_call(kernel, out_shape=(jax.ShapeDtypeStruct((1, rows), F32), j...  62.3 us
    pallas_call x1, Pallas kernels, on_device(): pl.pallas_call(lambda *refs: finish(scored, *refs), grid=(n_cut,), out_sh...  3 us

profile of v2, /device:TPU:1, one launch (start us, length us, event | category | flops | bytes accessed | tf_op | source)
XLA Modules:
  0.0 67.2 jit_solution(6242213243467989664)
XLA Ops:
  1.9 62.3 %shard_map.67 = (f32[1,128]{1,0:T(1,128)}, f32[128,1152]{1,0:T(8,128)}, f32[128,1152]{1,0:T(8,128)}) custom-call(f32[128,1152]{1,0:T(8,128)} %refs_0_.1, f32[128,1152]{1,0:T(8,128)} %refs_1_.1, f32[1]{0:T(128)S(6)} %copy.7.scale_ref.refs_5_, f32[1]{0:T(128)S(6)} %copy.8.bias_ref), custom_call_target="tpu_custom_call" | custom-call | flops 7247757312 | bytes 2359296 | tf_op jit(solution)/shard_map/pallas_call | solution.py:331
  64.2 3.0 %shard_map.68 = (f32[128]{0:T(128)}, f32[128,1152]{1,0:T(8,128)}, f32[128,1152]{1,0:T(8,128)}) custom-call(f32[128,1152]{1,0:T(8,128)} %refs_0_.1, f32[128,1152]{1,0:T(8,128)} %refs_1_.1, f32[128,1152]{1,0:T(8,128)} %get-tuple-element.6.refs_2_, f32[128,1152]{1,0:T(8,128)} %get-tuple-element.7.refs_3_, f32[1,128]{1,0:T(1,128)} %get-tuple-element.8.refs_4_, ...), custom_call_target="tpu_custom_call" | custom-call | tf_op jit(solution)/shard_map/pallas_call | solution.py:375

commit v3 on v2

--- a/solution.py
+++ b/solution.py
@@ -12,11 +12,10 @@
 
 CORES, RING = 2, 8
 N_AG = 2
-N_RS = 4
 N_T = 4
 SLOT = {1: 0, 7: 1, 2: 2, 6: 3, 3: 4, 5: 5, 4: 6, 0: 7}
-TURN = 4
-LANDS = {hop: n for n, hop in enumerate([*range(TURN + 1, RING + 1), *range(TURN - 1)])}
+TURNS = (4, 4, 4, 4)
+N_RS = len(TURNS)
 
 
 def column_dot(left, right):
@@ -29,10 +28,10 @@
 
 def kernel(
     image_ref, text_ref, scale_ref, bias_ref,
-    loss_ref, image_sum_ref, text_sum_ref,
-    raw_i, raw_t, img, txt, coef, part, tgrad, racc, sacc, rloss, sloss, losses,
+    loss_ref, image_grad_ref, text_grad_ref,
+    scalars, raw_i, raw_t, norm_i, norm_t, img, txt, coef, part, tgrad, racc, sacc, rloss, sloss, losses,
     sib_out, sib_in, d_out, d_in,
-    in_sem, ag_s, ag_r, t_r, f_s, rs_s, rs_r, l_s, l_r, sib_s, sib_r, d_s, d_r,
+    in_sem, out_sem, ag_s, ag_r, t_r, f_s, rs_s, rs_r, l_s, l_r, sib_s, sib_r, d_s, d_r,
 ):
     rows, embed = raw_i.shape
     n_grp = lax.axis_size("grp")
@@ -53,10 +52,21 @@
     barrier = pltpu.get_barrier_semaphore()
     for peer in (nxt, prv, sib, ypart, ahead, behind):
         pl.semaphore_signal(barrier, inc=1, device_id=peer, device_id_type=MESH)
-    fetch_i = pltpu.make_async_copy(image_ref, raw_i, in_sem.at[0])
-    fetch_t = pltpu.make_async_copy(text_ref, raw_t, in_sem.at[1])
-    fetch_i.start()
-    fetch_t.start()
+
+    def fetch(src, dst, n):
+        copy = pltpu.make_async_copy(src, dst, in_sem.at[n])
+        copy.start()
+        return copy
+
+    n_ag = rows // N_AG
+    fetch_i = [
+        fetch(image_ref.at[pl.ds(c * n_ag, n_ag)], raw_i.at[pl.ds(c * n_ag, n_ag)], c)
+        for c in range(N_AG)
+    ]
+    fetch_t = fetch(text_ref, raw_t, N_AG)
+    fetch_s = [
+        fetch(scale_ref, scalars.at[0], N_AG + 1), fetch(bias_ref, scalars.at[1], N_AG + 2)
+    ]
 
     sent = []
 
@@ -98,11 +108,18 @@
     def t_landed(slot, c):
         landed(t_rows(slot, c), t_r.at[slot, c])
 
-    def normalize(raw_ref, low):
+    def normalize(raw_ref, norm_ref, low):
         raw = raw_ref[...]
-        low[...] = (raw / row_norms(raw)).astype(BF16)
-
-    scale, bias = scale_ref[0], bias_ref[0]
+        norms = row_norms(raw)
+        norm_ref[...] = norms
+        low[...] = (raw / norms).astype(BF16)
+
+    def restore(raw_ref, norm_ref, at, unit_grad):
+        norms = norm_ref[at, :]
+        units = raw_ref[at, :] / norms
+        grad = scale * unit_grad
+        raw_ref[at, :] = (grad - units * jnp.sum(units * grad, axis=1, keepdims=True)) / norms
+
     wide = 2 * rows
 
     def images(u):
@@ -144,27 +161,26 @@
 
     def sum_on(hop, c):
         slot = SLOT[hop]
-        to, peer = (hop + 1, nxt) if hop >= TURN else (hop - 1, prv)
-        into, came = LANDS[to], LANDS.get(hop)
+        to, peer = (hop + 1, nxt) if hop >= TURNS[c] else (hop - 1, prv)
+        starts = hop in (TURNS[c], TURNS[c] - 1)
         n = rows // N_RS
         at = pl.ds(c * n, n)
         value = part[pl.ds(slot * rows + c * n, n), :]
-        if came is not None:
-            landed(racc.at[came, at], rs_r.at[came, c])
-            value = value + racc[came, at, :].astype(F32)
+        if not starts:
+            landed(racc.at[hop, at], rs_r.at[hop, c])
+            value = value + racc[hop, at, :].astype(F32)
         sacc[slot, at, :] = value.astype(BF16)
-        send(sacc.at[slot, at], racc.at[into, at], rs_s.at[slot, c], rs_r.at[into, c], peer)
+        send(sacc.at[slot, at], racc.at[to, at], rs_s.at[slot, c], rs_r.at[to, c], peer)
         if c == 0:
             mine = losses[:, pl.ds(slot * rows, rows)]
-            if came is not None:
-                landed(rloss.at[came], l_r.at[came])
-                mine = mine + rloss[came, 0:1, :]
+            if not starts:
+                landed(rloss.at[hop], l_r.at[hop])
+                mine = mine + rloss[hop, 0:1, :]
             sloss[slot] = jnp.broadcast_to(mine, (8, rows))
-            send(sloss.at[slot], rloss.at[into], l_s.at[slot], l_r.at[into], peer)
-
-    def sums_on(hop):
-        for c in range(N_RS):
-            sum_on(hop, c)
+            send(sloss.at[slot], rloss.at[to], l_s.at[slot], l_r.at[to], peer)
+
+    def ends(c):
+        return (0, RING) if TURNS[c] > 1 else (RING,)
 
     half = rows // 2
 
@@ -189,19 +205,24 @@
         at = t_half(s, h)
         tgrad[at, :] = tgrad[at, :] + d_in[m].astype(F32)
 
-    fetch_i.wait()
-    normalize(raw_i, img.at[pl.ds((RING - 1) * rows, rows)])
-    pl.semaphore_wait(barrier, 6)
     for c in range(N_AG):
+        fetch_i[c].wait()
+        at = pl.ds(c * n_ag, n_ag)
+        normalize(raw_i.at[at], norm_i.at[at], img_rows(0, c))
+        if c == 0:
+            pl.semaphore_wait(barrier, 6)
         ring_send(0, 1, c, nxt)
         ring_send(0, 7, c, prv)
     fetch_t.wait()
-    normalize(raw_t, txt.at[pl.ds(0, rows)])
+    normalize(raw_t, norm_t, txt.at[pl.ds(0, rows)])
     for c in range(N_T):
         t_send(0, c, 1, 1, ypart)
         t_send(0, (c + 2) % N_T, 2, 0, ahead)
     for c in range(N_T):
         t_send(0, c, 4, 2, sib)
+    for copy in fetch_s:
+        copy.wait()
+    scale, bias = scalars[0, 0], scalars[1, 0]
 
     def ring_on(hop, back, c):
         ring_chunk(hop, c)
@@ -252,113 +273,130 @@
     ring_on(3, 5, 1)
     score(2)
     image_part(2)
-    sums_on(3)
+    sum_on(3, 0)
+    sum_on(3, 1)
+    sum_on(3, 2)
+    sum_on(3, 3)
     ring_chunk(4, 0)
     ring_chunk(4, 1)
     score(3)
     image_part(3)
-    sums_on(4)
+    sum_on(4, 0)
+    sum_on(4, 1)
+    sum_on(4, 2)
+    sum_on(4, 3)
+    sum_on(2, 0)
     text_part(2, False)
+    sum_on(2, 1)
     text_part(3, False)
-    for s in (3, 2, 1, 0):
-        to_sib(s)
-    sums_on(2)
-    sums_on(5)
+    sum_on(2, 2)
+    sum_on(2, 3)
+    to_sib(3)
+    to_sib(2)
+    to_sib(1)
+    to_sib(0)
+    sum_on(5, 0)
     from_sib(3)
     d_send(0, 3, 0, behind)
     d_send(1, 3, 1, ypart)
+    sum_on(5, 1)
     from_sib(2)
     d_send(2, 2, 0, behind)
+    sum_on(5, 2)
     from_sib(1)
     d_send(3, 1, 1, ypart)
+    sum_on(5, 3)
     from_sib(0)
-    sums_on(1)
+    sum_on(1, 0)
+    sum_on(1, 1)
     d_add(1, 2, 1)
     d_send(4, 2, 1, behind)
-    sums_on(6)
+    sum_on(1, 2)
+    sum_on(1, 3)
     d_add(0, 1, 0)
     d_send(5, 1, 0, ypart)
+    sum_on(6, 0)
+    sum_on(6, 1)
     d_add(3, 0, 1)
+    sum_on(6, 2)
+    sum_on(6, 3)
     d_add(2, 0, 0)
-    sums_on(7)
+    sum_on(7, 0)
+    sum_on(7, 1)
     d_add(5, 0, 0)
+    sum_on(7, 2)
+    sum_on(7, 3)
     d_add(4, 0, 1)
-    text_sum_ref[...] = tgrad[pl.ds(0, rows), :]
-
+    restore(raw_t, norm_t, pl.ds(0, rows), tgrad[pl.ds(0, rows), :])
+    out = [pltpu.make_async_copy(raw_t, text_grad_ref, out_sem.at[0])]
+    out[0].start()
+    for copy in sent:
+        copy.wait_send()
     mine = losses[:, pl.ds(7 * rows, rows)]
-    for came in (LANDS[0], LANDS[8]):
+    for came in ends(0):
         landed(rloss.at[came], l_r.at[came])
         mine = mine + rloss[came, 0:1, :]
-    loss_ref[...] = mine
+    loss_ref[...] = mine / (STEPS * rows * lax.axis_size("ing"))
     n = rows // N_RS
     for c in range(N_RS):
         at = pl.ds(c * n, n)
         value = part[pl.ds(7 * rows + c * n, n), :]
-        for came in (LANDS[0], LANDS[8]):
+        for came in ends(c):
             landed(racc.at[came, at], rs_r.at[came, c])
             value = value + racc[came, at, :].astype(F32)
-        image_sum_ref[at, :] = value
-    for copy in sent:
-        copy.wait_send()
-
-
-def finish(scored, image_ref, text_ref, image_sum_ref, text_sum_ref, loss_sum_ref, scale_ref,
-           loss_ref, image_grad_ref, text_grad_ref):
-    scale = scale_ref[0]
-
-    def restore(raw_ref, sum_ref, out_ref):
-        raw = raw_ref[...]
-        norms = row_norms(raw)
-        units = raw / norms
-        grad = scale * sum_ref[...]
-        out_ref[...] = (grad - units * jnp.sum(units * grad, axis=1, keepdims=True)) / norms
-
-    restore(image_ref, image_sum_ref, image_grad_ref)
-    restore(text_ref, text_sum_ref, text_grad_ref)
-
-    @pl.when(pl.program_id(0) == 0)
-    def _():
-        loss_ref[...] = loss_sum_ref[0, :] / scored
+        restore(raw_i, norm_i, at, value)
+        out.append(pltpu.make_async_copy(raw_i.at[at], image_grad_ref.at[at], out_sem.at[1 + c]))
+        out[-1].start()
+    for copy in out:
+        copy.wait()
+
+
+def finish(image_in_ref, text_in_ref, loss_in_ref, loss_ref, image_grad_ref, text_grad_ref):
+    image_grad_ref[...] = image_in_ref[...]
+    text_grad_ref[...] = text_in_ref[...]
+    loss_ref[...] = loss_in_ref[0, :]
 
 
 def on_device(image_emb, text_emb, logit_scale, logit_bias):
     rows, embed = image_emb.shape
     full, dma = RING * rows, pltpu.SemaphoreType.DMA
     wide, half = 2 * rows, rows // 2
-    whole, smem = pl.BlockSpec(memory_space=pltpu.VMEM), pl.BlockSpec(memory_space=pltpu.SMEM)
-    far = pl.BlockSpec(memory_space=pl.ANY)
+    whole, far = pl.BlockSpec(memory_space=pltpu.VMEM), pl.BlockSpec(memory_space=pltpu.HBM)
     vmem = pltpu.VMEM
-    loss_sum, image_sum, text_sum = pl.pallas_call(
+    loss, image_grad, text_grad = pl.pallas_call(
         kernel,
         out_shape=(
             jax.ShapeDtypeStruct((1, rows), F32),
             jax.ShapeDtypeStruct((rows, embed), F32),
             jax.ShapeDtypeStruct((rows, embed), F32),
         ),
-        in_specs=[far, far, smem, smem],
-        out_specs=(whole, whole, whole),
+        in_specs=[far, far, far, far],
+        out_specs=(whole, far, far),
         scratch_shapes=[
+            pltpu.SMEM((2, 1), F32),
             vmem((rows, embed), F32),
             vmem((rows, embed), F32),
+            vmem((rows, 1), F32),
+            vmem((rows, 1), F32),
             vmem((full, embed), BF16),
             vmem((full, embed), BF16),
             vmem((4, full, wide), BF16),
             vmem((full, embed), F32),
             vmem((full, embed), F32),
+            vmem((RING + 1, rows, embed), BF16),
             vmem((7, rows, embed), BF16),
-            vmem((7, rows, embed), BF16),
-            vmem((7, 8, rows), F32),
+            vmem((RING + 1, 8, rows), F32),
             vmem((7, 8, rows), F32),
             vmem((1, full), F32),
             vmem((4, rows, embed), BF16),
             vmem((4, rows, embed), BF16),
             vmem((6, half, embed), BF16),
             vmem((6, half, embed), BF16),
-            dma((2,)),
+            dma((N_AG + 3,)), dma((1 + N_RS,)),
             dma((7, N_AG)), dma((7, N_AG)),
             dma((8, N_T)), dma((7, N_T)),
-            dma((7, N_RS)), dma((7, N_RS)),
-            dma((7,)), dma((7,)),
+            dma((7, N_RS)), dma((RING + 1, N_RS)),
+            dma((7,)), dma((RING + 1,)),
             dma((4,)), dma((4,)),
             dma((6,)), dma((6,)),
         ],
@@ -369,20 +407,19 @@
             flops=6 * full * full * embed, bytes_accessed=16 * rows * embed, transcendentals=3 * full * full
         ),
     )(image_emb, text_emb, logit_scale, logit_bias)
-    n_cut = 1
+    n_cut = 2
     tile = pl.BlockSpec((rows // n_cut, embed), lambda n: (n, 0))
-    scored = STEPS * rows * lax.axis_size("ing")
     return pl.pallas_call(
-        lambda *refs: finish(scored, *refs),
+        finish,
         grid=(n_cut,),
         out_shape=(
             jax.ShapeDtypeStruct((rows,), F32),
             jax.ShapeDtypeStruct((rows, embed), F32),
             jax.ShapeDtypeStruct((rows, embed), F32),
         ),
-        in_specs=[tile, tile, tile, tile, pl.BlockSpec((1, rows), lambda n: (0, 0)), smem],
+        in_specs=[tile, tile, pl.BlockSpec((1, rows), lambda n: (0, 0))],
         out_specs=(pl.BlockSpec((rows,), lambda n: (0,)), tile, tile),
-    )(image_emb, text_emb, image_sum, text_sum, loss_sum, logit_scale)
+    )(image_grad, text_grad, loss)
 
 
 def solution(mesh):

time: 68.3 us -> 66.8 us (0.978); the launches traced: 67.2 us -> 66.7 us
    pallas_call x1, Pallas kernels: 3 us -> 2.12 us  [on_device(): pl.pallas_call(finish, grid=(n_cut,), out_shape=(jax.ShapeDtypeStruct((ro...]
where the time goes in v3:
time: 66.8 us; the launch traced here: 66.7 us
  Pallas kernels  64.7 us (97%)
  between operations  1.93 us (3%)
    pallas_call x1, Pallas kernels, on_device(): pl.pallas_call(kernel, out_shape=(jax.ShapeDtypeStruct((1, rows), F32), j...  62.6 us
    pallas_call x1, Pallas kernels, on_device(): pl.pallas_call(finish, grid=(n_cut,), out_shape=(jax.ShapeDtypeStruct((ro...  2.12 us

profile of v3, /device:TPU:1, one launch (start us, length us, event | category | flops | bytes accessed | tf_op | source)
XLA Modules:
  0.0 66.7 jit_solution(14318380247446991026)
XLA Ops:
  1.9 62.6 %shard_map.67 = (f32[1,128]{1,0:T(1,128)}, f32[128,1152]{1,0:T(8,128)}, f32[128,1152]{1,0:T(8,128)}) custom-call(f32[128,1152]{1,0:T(8,128)} %image_ref.1, f32[128,1152]{1,0:T(8,128)} %text_ref.1, f32[1]{0:T(128)S(6)} %copy.7.scale_ref, f32[1]{0:T(128)S(6)} %copy.8.bias_ref), custom_call_target="tpu_custom_call" | custom-call | flops 7247757312 | bytes 2359296 | tf_op jit(solution)/shard_map/pallas_call | solution.py:366
  64.5 2.1 %shard_map.68 = (f32[128]{0:T(128)}, f32[128,1152]{1,0:T(8,128)}, f32[128,1152]{1,0:T(8,128)}) custom-call(f32[128,1152]{1,0:T(8,128)} %get-tuple-element.6.image_in_ref, f32[128,1152]{1,0:T(8,128)} %get-tuple-element.7.text_in_ref, f32[1,128]{1,0:T(1,128)} %get-tuple-element.8.loss_in_ref), custom_call_target="tpu_custom_call" | custom-call | tf_op jit(solution)/shard_map/pallas_call | solution.py:412

commit v4 on v3

--- a/solution.py
+++ b/solution.py
@@ -11,7 +11,7 @@
 F32, BF16 = jnp.float32, jnp.bfloat16
 
 CORES, RING = 2, 8
-N_AG = 2
+N_AG = 4
 N_T = 4
 SLOT = {1: 0, 7: 1, 2: 2, 6: 3, 3: 4, 5: 5, 4: 6, 0: 7}
 TURNS = (4, 4, 4, 4)
@@ -31,7 +31,7 @@
     loss_ref, image_grad_ref, text_grad_ref,
     scalars, raw_i, raw_t, norm_i, norm_t, img, txt, coef, part, tgrad, racc, sacc, rloss, sloss, losses,
     sib_out, sib_in, d_out, d_in,
-    in_sem, out_sem, ag_s, ag_r, t_r, f_s, rs_s, rs_r, l_s, l_r, sib_s, sib_r, d_s, d_r,
+    in_sem, ag_s, ag_r, t_r, f_s, rs_s, rs_r, l_s, l_r, sib_s, sib_r, d_s, d_r,
 ):
     rows, embed = raw_i.shape
     n_grp = lax.axis_size("grp")
@@ -114,45 +114,47 @@
         norm_ref[...] = norms
         low[...] = (raw / norms).astype(BF16)
 
-    def restore(raw_ref, norm_ref, at, unit_grad):
+    def restore(raw_ref, norm_ref, grad_ref, at, unit_grad):
         norms = norm_ref[at, :]
         units = raw_ref[at, :] / norms
         grad = scale * unit_grad
-        raw_ref[at, :] = (grad - units * jnp.sum(units * grad, axis=1, keepdims=True)) / norms
+        grad_ref[at, :] = (grad - units * jnp.sum(units * grad, axis=1, keepdims=True)) / norms
 
     wide = 2 * rows
 
-    def images(u):
-        return pl.ds(u * wide, wide)
-
-    def score(u):
-        dots = column_dot(txt[...], img[images(u), :])
-        x = scale * dots + bias
+    def images(u, lo=0, hi=2):
+        return pl.ds((2 * u + lo) * rows, (hi - lo) * rows)
+
+    def score(u, lo=0, hi=2):
+        at, columns = images(u, lo, hi), pl.ds(lo * rows, (hi - lo) * rows)
+        x = scale * column_dot(txt[...], img[at, :]) + bias
         e = jnp.exp(x)
         one = 1.0 + e
         inv = pl.reciprocal(one, approx=True)
         inv = inv * (2.0 - one * inv)
         loss = jnp.log(one) + (e - (one - 1.0)) * inv
-        coef[u] = (e * inv).astype(BF16)
-        losses[:, images(u)] = jnp.sum(loss, axis=0, keepdims=True)
-        if u == 3:
-            x = x[:rows, rows:]
+        coef[u, :, columns] = (e * inv).astype(BF16)
+        losses[:, at] = jnp.sum(loss, axis=0, keepdims=True)
+        if (u, hi) == (3, 2):
+            mine = (hi - lo - 1) * rows
+            x = x[:rows, mine:]
             own = lax.broadcasted_iota(jnp.int32, x.shape, 0) == lax.broadcasted_iota(
                 jnp.int32, x.shape, 1
             )
             m = jnp.exp(-jnp.abs(x))
             one_m = 1.0 + m
             pair = jnp.log(one_m) + (m - (one_m - 1.0)) / one_m + jnp.maximum(-x, 0.0)
-            inv = inv[:rows, rows:]
-            coef[u, :rows, rows:] = jnp.where(own, -inv, e[:rows, rows:] * inv).astype(BF16)
+            inv = inv[:rows, mine:]
+            coef[u, :rows, rows:] = jnp.where(own, -inv, e[:rows, mine:] * inv).astype(BF16)
             loss = jnp.concatenate(
-                [jnp.where(own, pair, loss[:rows, rows:]), loss[rows:, rows:]], axis=0
+                [jnp.where(own, pair, loss[:rows, mine:]), loss[rows:, mine:]], axis=0
             )
             losses[:, pl.ds(7 * rows, rows)] = jnp.sum(loss, axis=0, keepdims=True)
 
-    def image_part(u):
-        part[images(u), :] = lax.dot_general(
-            coef[u], txt[...], (((0,), (0,)), ((), ())), preferred_element_type=F32
+    def image_part(u, lo=0, hi=2):
+        part[images(u, lo, hi), :] = lax.dot_general(
+            coef[u, :, lo * rows : hi * rows], txt[...], (((0,), (0,)), ((), ())),
+            preferred_element_type=F32,
         )
 
     def text_part(u, first):
@@ -248,49 +250,61 @@
     behind_text(2)
     partner_text(1)
     ring_on(1, 7, 0)
+    ring_on(1, 7, 1)
     behind_text(3)
     partner_text(2)
     behind_text(0)
     partner_text(3)
-    ring_on(1, 7, 1)
+    ring_on(1, 7, 2)
+    ring_on(1, 7, 3)
     behind_text(1)
     far_text(2)
     far_text(0)
     far_text(3)
     ring_on(2, 6, 0)
+    ring_on(2, 6, 1)
     far_text(1)
     for slot in range(4, 8):
         for c in range(N_T):
             t_landed(slot, c)
     score(0)
-    ring_on(2, 6, 1)
+    ring_on(2, 6, 2)
+    ring_on(2, 6, 3)
     score(1)
     image_part(1)
     ring_on(3, 5, 0)
+    ring_on(3, 5, 1)
     text_part(1, True)
     image_part(0)
     text_part(0, False)
-    ring_on(3, 5, 1)
-    score(2)
-    image_part(2)
+    ring_on(3, 5, 2)
+    ring_on(3, 5, 3)
+    score(2, 0, 1)
+    image_part(2, 0, 1)
     sum_on(3, 0)
     sum_on(3, 1)
     sum_on(3, 2)
     sum_on(3, 3)
+    score(2, 1, 2)
     ring_chunk(4, 0)
     ring_chunk(4, 1)
-    score(3)
-    image_part(3)
+    ring_chunk(4, 2)
+    ring_chunk(4, 3)
+    score(3, 0, 1)
+    image_part(3, 0, 1)
     sum_on(4, 0)
     sum_on(4, 1)
     sum_on(4, 2)
     sum_on(4, 3)
+    score(3, 1, 2)
+    text_part(2, False)
     sum_on(2, 0)
-    text_part(2, False)
     sum_on(2, 1)
-    text_part(3, False)
     sum_on(2, 2)
     sum_on(2, 3)
+    text_part(3, False)
+    image_part(2, 1, 2)
+    image_part(3, 1, 2)
     to_sib(3)
     to_sib(2)
     to_sib(1)
@@ -327,16 +341,14 @@
     sum_on(7, 2)
     sum_on(7, 3)
     d_add(4, 0, 1)
-    restore(raw_t, norm_t, pl.ds(0, rows), tgrad[pl.ds(0, rows), :])
-    out = [pltpu.make_async_copy(raw_t, text_grad_ref, out_sem.at[0])]
-    out[0].start()
+    restore(raw_t, norm_t, text_grad_ref, pl.ds(0, rows), tgrad[pl.ds(0, rows), :])
     for copy in sent:
         copy.wait_send()
     mine = losses[:, pl.ds(7 * rows, rows)]
     for came in ends(0):
         landed(rloss.at[came], l_r.at[came])
         mine = mine + rloss[came, 0:1, :]
-    loss_ref[...] = mine / (STEPS * rows * lax.axis_size("ing"))
+    loss_ref[...] = mine[0, :] / (STEPS * rows * lax.axis_size("ing"))
     n = rows // N_RS
     for c in range(N_RS):
         at = pl.ds(c * n, n)
@@ -344,17 +356,17 @@
         for came in ends(c):
             landed(racc.at[came, at], rs_r.at[came, c])
             value = value + racc[came, at, :].astype(F32)
-        restore(raw_i, norm_i, at, value)
-        out.append(pltpu.make_async_copy(raw_i.at[at], image_grad_ref.at[at], out_sem.at[1 + c]))
-        out[-1].start()
-    for copy in out:
-        copy.wait()
-
-
-def finish(image_in_ref, text_in_ref, loss_in_ref, loss_ref, image_grad_ref, text_grad_ref):
-    image_grad_ref[...] = image_in_ref[...]
-    text_grad_ref[...] = text_in_ref[...]
+        restore(raw_i, norm_i, image_grad_ref, at, value)
+
+
+def finish(image_in_ref, text_in_ref, loss_in_ref, loss_ref, image_grad_ref, text_grad_ref, sem):
+    image = pltpu.make_async_copy(image_in_ref, image_grad_ref, sem.at[0])
+    text = pltpu.make_async_copy(text_in_ref, text_grad_ref, sem.at[1])
+    image.start()
+    text.start()
     loss_ref[...] = loss_in_ref[0, :]
+    image.wait()
+    text.wait()
 
 
 def on_device(image_emb, text_emb, logit_scale, logit_bias):
@@ -365,13 +377,9 @@
     vmem = pltpu.VMEM
     loss, image_grad, text_grad = pl.pallas_call(
         kernel,
-        out_shape=(
-            jax.ShapeDtypeStruct((1, rows), F32),
-            jax.ShapeDtypeStruct((rows, embed), F32),
-            jax.ShapeDtypeStruct((rows, embed), F32),
-        ),
+        out_shape=(vmem((rows,), F32), vmem((rows, embed), F32), vmem((rows, embed), F32)),
         in_specs=[far, far, far, far],
-        out_specs=(whole, far, far),
+        out_specs=(whole, whole, whole),
         scratch_shapes=[
             pltpu.SMEM((2, 1), F32),
             vmem((rows, embed), F32),
@@ -392,7 +400,7 @@
             vmem((4, rows, embed), BF16),
             vmem((6, half, embed), BF16),
             vmem((6, half, embed), BF16),
-            dma((N_AG + 3,)), dma((1 + N_RS,)),
+            dma((N_AG + 3,)),
             dma((7, N_AG)), dma((7, N_AG)),
             dma((8, N_T)), dma((7, N_T)),
             dma((7, N_RS)), dma((RING + 1, N_RS)),
@@ -407,19 +415,7 @@
             flops=6 * full * full * embed, bytes_accessed=16 * rows * embed, transcendentals=3 * full * full
         ),
     )(image_emb, text_emb, logit_scale, logit_bias)
-    n_cut = 2
-    tile = pl.BlockSpec((rows // n_cut, embed), lambda n: (n, 0))
-    return pl.pallas_call(
-        finish,
-        grid=(n_cut,),
-        out_shape=(
-            jax.ShapeDtypeStruct((rows,), F32),
-            jax.ShapeDtypeStruct((rows, embed), F32),
-            jax.ShapeDtypeStruct((rows, embed), F32),
-        ),
-        in_specs=[tile, tile, pl.BlockSpec((1, rows), lambda n: (0, 0))],
-        out_specs=(pl.BlockSpec((rows,), lambda n: (0,)), tile, tile),
-    )(image_grad, text_grad, loss)
+    return loss, image_grad, text_grad
 
 
 def solution(mesh):

time: 66.8 us -> 64.8 us (0.970)
  Pallas kernels: 64.7 us -> 60.5 us
  local copies, waits for them, and re-layouts: 0 us -> 2.14 us
    pallas_call x2 -> x1, Pallas kernels: 64.7 us -> 60.5 us  [on_device(): pl.pallas_call(kernel, out_shape=(vmem((rows,), F32), vmem((rows, embed),...]
    unnamed x0 -> x3, local copies, waits for them, and re-layouts: none -> 2.14 us
where the time goes in v4:
time: 64.8 us; the launch traced here: 64.5 us
  Pallas kernels  60.5 us (93%)
  local copies, waits for them, and re-layouts  2.14 us (3%)
  between operations  1.93 us (3%)
    pallas_call x1, Pallas kernels, on_device(): pl.pallas_call(kernel, out_shape=(vmem((rows,), F32), vmem((rows, embed),...  60.5 us
    unnamed x3, local copies, waits for them, and re-layouts  2.14 us

profile of v4, /device:TPU:1, one launch (start us, length us, event | category | flops | bytes accessed | tf_op | source)
XLA Modules:
  0.0 64.5 jit_solution(15096025069566988489)
XLA Ops:
  1.9 60.5 %shard_map.67 = (f32[128]{0:T(128)S(1)}, f32[128,1152]{1,0:T(8,128)S(1)}, f32[128,1152]{1,0:T(8,128)S(1)}) custom-call(f32[128,1152]{1,0:T(8,128)} %image_ref.1, f32[128,1152]{1,0:T(8,128)} %text_ref.1, f32[1]{0:T(128)S(6)} %copy.13.scale_ref, f32[1]{0:T(128)S(6)} %copy.14.bias_ref), custom_call_target="tpu_custom_call" | custom-call | flops 7247757312 | bytes 2359296 | tf_op jit(solution)/shard_map/pallas_call | solution.py:378
  62.4 0.5 copy.10
  62.9 0.8 %copy.11 = f32[128,1152]{1,0:T(8,128)} copy(f32[128,1152]{1,0:T(8,128)S(1)} %get-tuple-element.4) | data formatting | bytes 1179648
  63.7 0.8 %copy.12 = f32[128,1152]{1,0:T(8,128)} copy(f32[128,1152]{1,0:T(8,128)S(1)} %get-tuple-element.5) | data formatting | bytes 1179648

commit v5 on v4

--- a/solution.py
+++ b/solution.py
@@ -274,9 +274,7 @@
     image_part(1)
     ring_on(3, 5, 0)
     ring_on(3, 5, 1)
-    text_part(1, True)
     image_part(0)
-    text_part(0, False)
     ring_on(3, 5, 2)
     ring_on(3, 5, 3)
     score(2, 0, 1)
@@ -286,6 +284,7 @@
     sum_on(3, 2)
     sum_on(3, 3)
     score(2, 1, 2)
+    text_part(1, True)
     ring_chunk(4, 0)
     ring_chunk(4, 1)
     ring_chunk(4, 2)
@@ -297,13 +296,14 @@
     sum_on(4, 2)
     sum_on(4, 3)
     score(3, 1, 2)
-    text_part(2, False)
+    text_part(0, False)
     sum_on(2, 0)
     sum_on(2, 1)
     sum_on(2, 2)
     sum_on(2, 3)
+    text_part(2, False)
+    image_part(2, 1, 2)
     text_part(3, False)
-    image_part(2, 1, 2)
     image_part(3, 1, 2)
     to_sib(3)
     to_sib(2)

time: 64.8 us -> 64.9 us (level)
  no operation moved by 1% of the time
where the time goes in v5:
time: 64.9 us; the launch traced here: 64.8 us
  Pallas kernels  60.7 us (94%)
  local copies, waits for them, and re-layouts  2.14 us (3%)
  between operations  1.93 us (3%)
    pallas_call x1, Pallas kernels, on_device(): pl.pallas_call(kernel, out_shape=(vmem((rows,), F32), vmem((rows, embed),...  60.7 us
    unnamed x3, local copies, waits for them, and re-layouts  2.14 us

profile of v5, /device:TPU:1, one launch (start us, length us, event | category | flops | bytes accessed | tf_op | source)
XLA Modules:
  0.0 64.8 jit_solution(14035543271535547315)
XLA Ops:
  1.9 60.7 %shard_map.67 = (f32[128]{0:T(128)S(1)}, f32[128,1152]{1,0:T(8,128)S(1)}, f32[128,1152]{1,0:T(8,128)S(1)}) custom-call(f32[128,1152]{1,0:T(8,128)} %image_ref.1, f32[128,1152]{1,0:T(8,128)} %text_ref.1, f32[1]{0:T(128)S(6)} %copy.13.scale_ref, f32[1]{0:T(128)S(6)} %copy.14.bias_ref), custom_call_target="tpu_custom_call" | custom-call | flops 7247757312 | bytes 2359296 | tf_op jit(solution)/shard_map/pallas_call | solution.py:378
  62.7 0.5 copy.10
  63.2 0.8 %copy.11 = f32[128,1152]{1,0:T(8,128)} copy(f32[128,1152]{1,0:T(8,128)S(1)} %get-tuple-element.4) | data formatting | bytes 1179648
  64.0 0.8 %copy.12 = f32[128,1152]{1,0:T(8,128)} copy(f32[128,1152]{1,0:T(8,128)S(1)} %get-tuple-element.5) | data formatting | bytes 1179648
